TPU v7x, 32 devices: a whole 2x2x4 slice. The times are simulated.
32 devices in a mesh: area: 8 (over z, x), col: 4 (over y, core).
Axes of the slice: x: 2, y: 2, z: 4, core: 2. Of those that a mesh axis runs over, the one named last changes fastest.
Arguments:
- initial_state: float32 [256, 128, 128], P(('area', 'col')), may hold values from -6 to 6
- past_rates: bfloat16 [2, 256, 128, 128], P(None, ('area', 'col')), may hold values from 0 to 2
- stimulus: bfloat16 [256, 128, 128], P(('area', 'col')), may hold values from -6 to 6
- leak_rate: float32 [256, 128], P(('area', 'col')), may hold values from 0.05 to 0.5
- local_weight: bfloat16 [256, 12, 128, 128], P(('area', 'col')), may hold values from -0.125 to 0.125
- far_weight: bfloat16 [256, 8, 128, 128], P(('area', 'col')), may hold values from -0.125 to 0.125
- local_index: int32 [256, 12], P(('area', 'col')), may hold values from 0 to 31, all different within a row
- area_sizes: int32 [4], replicated, may hold values from 1 to 3, as said below
- far_area: int32 [256, 8], replicated, may hold values from 0 to 3, as said below
- far_offset: int32 [256, 8], replicated, may hold values from 0 to 95, as said below
Outputs:
- final_state: float32 [256, 128, 128], P(('area', 'col'))
Inputs may be any that keep to these rules, and one draw needn't show every extreme that they name: `area_sizes`: Areas' section counts sum to 8; some area has exactly 3 sections. `far_area`: the source area of a far link differs from the area that holds its block row. In each aligned group of 8 block rows, at most 16 far links read blocks of one section (blocks s * 32 to s * 32 + 31), and exactly 16 read some section. `far_offset`: each offset lies below its source area's sections times 32.
All inputs are finite; a program needn't handle non-finite values.
Results may differ from a plain program's by a relative error of at most 0.0009.
Values may be sent and summed in bfloat16 or wider, within the bound.
A program may use at most 128 MiB of HBM per device.

v0:
```python
import jax
import jax.numpy as jnp
from jax import lax
from jax.sharding import PartitionSpec as P

STEPS = 4


def shards(
    initial_state,
    past_rates,
    stimulus,
    leak_rate,
    local_weight,
    far_weight,
    local_index,
    area_sizes,
    far_area,
    far_offset,
):
    area_count = lax.axis_size("area")
    col_count = lax.axis_size("col")
    my_area = lax.axis_index("area")
    my_col = lax.axis_index("col")
    row_count = initial_state.shape[0]
    trial_count = initial_state.shape[1]
    block_len = initial_state.shape[2]
    link_count = row_count * far_weight.shape[1]
    slot_count = 2 * link_count // area_count
    section_len = row_count * col_count
    delay_len = past_rates.shape[0]
    area_ids = jnp.arange(area_sizes.shape[0], dtype=jnp.int32)
    starts = jnp.cumsum(area_sizes) - area_sizes
    match_area = far_area[..., None] == area_ids
    area_len = jnp.sum(jnp.where(match_area, area_sizes, 0), axis=-1)
    area_first = jnp.sum(jnp.where(match_area, starts, 0), axis=-1)
    far_block = area_first * section_len + far_offset % (area_len * section_len)
    by_device = far_block.reshape(area_count, col_count, link_count)
    same_col = lax.dynamic_index_in_dim(by_device, my_col, axis=1, keepdims=False)
    section_of = same_col // section_len
    placing = same_col % section_len
    earlier = jnp.tril(jnp.ones((link_count, link_count), jnp.bool_), -1)
    order_rank = jnp.sum(
        (section_of[:, :, None] == section_of[:, None, :]) & earlier[None], axis=-1
    )
    slot_ids = jnp.arange(slot_count, dtype=order_rank.dtype)
    wanted = (section_of[:, None, :] == my_area) & (
        order_rank[:, None, :] == slot_ids[None, :, None]
    )
    slot_place = jnp.sum(jnp.where(wanted, placing[:, None, :], 0), axis=-1).reshape(-1)
    slot_used = jnp.any(wanted, axis=-1).reshape(-1)
    own_section = lax.dynamic_index_in_dim(section_of, my_area, axis=0, keepdims=False)
    own_rank = lax.dynamic_index_in_dim(order_rank, my_area, axis=0, keepdims=False)
    arrival = own_section * slot_count + own_rank
    leak_gain = leak_rate[:, None, :]
    drive_term = stimulus.astype(jnp.float32)
    membrane = initial_state
    rate_now = jax.nn.softplus(membrane).astype(jnp.bfloat16)
    sections = []
    for step_idx in range(STEPS):
        section = lax.all_gather(rate_now, "col", axis=0, tiled=True)
        sections.append(section)
        if step_idx < delay_len:
            source = lax.all_gather(past_rates[step_idx], "col", axis=0, tiled=True)
        else:
            source = sections[step_idx - delay_len]
        frames = source[None]
        picked = frames[:, slot_place]
        arrived = lax.all_to_all(
            jnp.where(slot_used[None, :, None, None], picked, jnp.zeros((), frames.dtype)),
            "area",
            split_axis=1,
            concat_axis=1,
            tiled=True,
        )[0]
        lateral = jnp.einsum(
            "rktb,rkob->rto", section[local_index], local_weight, preferred_element_type=jnp.float32
        )
        distant = jnp.einsum(
            "rktb,rkob->rto",
            arrived[arrival].reshape(row_count, -1, trial_count, block_len),
            far_weight,
            preferred_element_type=jnp.float32,
        )
        membrane = membrane + leak_gain * (-membrane + lateral + distant + drive_term)
        if step_idx + 1 < STEPS:
            rate_now = jax.nn.softplus(membrane).astype(jnp.bfloat16)
    return membrane


def solution(mesh):
    return jax.shard_map(
        shards,
        mesh=mesh,
        in_specs=(
            P(("area", "col"), None, None),
            P(None, ("area", "col"), None, None),
            P(("area", "col"), None, None),
            P(("area", "col"), None),
            P(("area", "col"), None, None, None),
            P(("area", "col"), None, None, None),
            P(("area", "col"), None),
            P(),
            P(),
            P(),
        ),
        out_specs=P(("area", "col"), None, None),
        check_vma=False,
    )
```

profile of v0, /device:TPU:25, one launch (start us, length us, event | category | flops | bytes accessed | tf_op | source)
XLA Modules:
  0.0 485.2 jit_solution(18126579920330529867)
XLA Ops:
  6.5 0.0 copy-start
  6.5 2.0 slice_bitcast_fusion
  8.6 0.0 all-gather.17.cloned.1.call-update
  8.6 0.8 reduce-window.9
  9.4 0.7 bitcast_subtract_fusion
  10.1 0.8 select_reduce_fusion.1
  10.9 0.8 fusion.30
  11.7 0.1 copy.24
  11.8 0.1 reshape.186
  12.0 0.1 iota_compare_fusion.1
  12.1 0.3 convert_reduce_fusion
  12.4 0.2 select_reduce_fusion
  12.7 0.1 reshape.187
  12.7 0.2 fusion.29
  13.0 0.1 broadcast_in_dim.100
  13.1 14.0 %all-gather.17.cloned.1.call-done = bf16[1,32,128,128]{3,2,0,1:T(8,128)(2,1)} async-done(((bf16[1,8,128,128]{3,2,0,1:T(8,128)(2,1)}), bf16[1,32,128,128]{3,2,0,1:T(8,128)(2,1)}) %all-gather.17.cloned.1.call-update) | async-done | bytes 1048592 | tf_op jit(solution)/shard_map/all_gather | solution.py:64
  27.1 4.3 gather_fusion.1
  31.3 4.5 fusion.3
  35.9 5.6 %all-to-all-start = ((bf16[1,128,128,128]{3,2,0,1:T(8,128)(2,1)}), bf16[1,128,128,128]{3,2,0,1:T(8,128)(2,1)}, u32[]{:S(2)}, u32[]{:S(2)}) async-start(bf16[1,128,128,128]{3,2,0,1:T(8,128)(2,1)} %fusion.3), calls=%async_computation | async-start | bytes 8388608 | tf_op jit(solution)/shard_map/all_to_all | solution.py:69
  41.5 2.0 fusion.24
  43.5 0.0 all-gather.9.cloned.1.call-update
  43.5 0.0 all-gather.19.cloned.1.call-start
  43.6 0.7 all-gather.19.cloned.1.call-update
  44.3 0.0 all-gather.11.cloned.1.call-start
  44.3 0.0 copy-done.6
  44.3 0.1 reshape.194
  44.4 16.7 %all-gather.9.cloned.1.call-done = bf16[32,128,128]{2,1,0:T(8,128)(2,1)} async-done(((bf16[8,128,128]{2,1,0:T(8,128)(2,1)}), bf16[32,128,128]{2,1,0:T(8,128)(2,1)}) %all-gather.9.cloned.1.call-update) | async-done | bytes 1048592 | tf_op jit(solution)/shard_map/all_gather | solution.py:61
  61.2 4.0 gather_fusion
  65.1 68.8 %all-to-all-done = bf16[1,128,128,128]{3,2,0,1:T(8,128)(2,1)} async-done(((bf16[1,128,128,128]{3,2,0,1:T(8,128)(2,1)}), bf16[1,128,128,128]{3,2,0,1:T(8,128)(2,1)}, u32[]{:S(2)}, u32[]{:S(2)}) %all-to-all-start) | async-done | bytes 4194336 | tf_op jit(solution)/shard_map/all_to_all | solution.py:69
  133.9 4.4 gather_fusion.2
  138.3 3.1 convolution_bitcast_fusion.6
  141.4 0.0 copy-done.1
  141.4 0.1 copy-done.3
  141.5 0.1 copy-done.4
  141.6 2.0 fusion.25
  143.6 0.0 all-gather.11.cloned.1.call-update
  143.6 0.0 all-gather.19.cloned.1.call-done
  143.7 4.3 gather_fusion.4
  147.9 4.3 gather_fusion.7
  152.2 7.7 %all-gather.11.cloned.1.call-done = bf16[32,128,128]{2,1,0:T(8,128)(2,1)} async-done(((bf16[8,128,128]{2,1,0:T(8,128)(2,1)}), bf16[32,128,128]{2,1,0:T(8,128)(2,1)}) %all-gather.11.cloned.1.call-update) | async-done | bytes 1048592 | tf_op jit(solution)/shard_map/all_gather | solution.py:61
  159.9 4.2 gather_fusion.10
  164.1 7.0 %fusion = (bf16[1,128,128,128]{3,2,0,1:T(8,128)(2,1)}, bf16[1,128,128,128]{3,2,0,1:T(8,128)(2,1)S(1)}, bf16[1,128,128,128]{3,2,0,1:T(8,128)(2,1)S(1)}) fusion(bf16[128,128,128]{2,1,0:T(8,128)(2,1)} %gather_fusion.10, pred[128]{0:T(512)(128)(4,1)S(1)} %broadcast_in_dim.100, bf16[128,128,128]{2,1,0:T(8,128)(2,1)} %gather_fusion.4, ...), kind=kLoop, calls=%fused_computation.13 | loop fusion | flops 6291456 | bytes 25165952 | tf_op jit(solution)/shard_map/jit(_where)/select_n | solution.py:70
  171.2 96.1 %all_to_all.20 = bf16[1,128,128,128]{3,2,0,1:T(8,128)(2,1)} all-to-all(bf16[1,128,128,128]{3,2,0,1:T(8,128)(2,1)S(1)} %get-tuple-element.14), channel_id=1, replica_groups=mesh['area'=8,'col'=4] {'area'}, dimensions={1} | all-to-all | bytes 8388608 | tf_op jit(solution)/shard_map/all_to_all | solution.py:69
  267.2 96.5 %all_to_all.21 = bf16[1,128,128,128]{3,2,0,1:T(8,128)(2,1)} all-to-all(bf16[1,128,128,128]{3,2,0,1:T(8,128)(2,1)S(1)} %get-tuple-element.15), channel_id=1, replica_groups=mesh['area'=8,'col'=4] {'area'}, dimensions={1} | all-to-all | bytes 8388608 | tf_op jit(solution)/shard_map/all_to_all | solution.py:69
  363.7 6.2 %all-to-all-start.3 = ((bf16[1,128,128,128]{3,2,0,1:T(8,128)(2,1)}), bf16[1,128,128,128]{3,2,0,1:T(8,128)(2,1)}, u32[]{:S(2)}, u32[]{:S(2)}) async-start(bf16[1,128,128,128]{3,2,0,1:T(8,128)(2,1)} %get-tuple-element.13), calls=%async_computation.3 | async-start | bytes 8388608 | tf_op jit(solution)/shard_map/all_to_all | solution.py:69
  369.9 3.9 gather_fusion.3
  373.8 4.4 gather_fusion.5
  378.2 3.1 convolution_bitcast_fusion.4
  381.3 0.1 copy-done.2
  381.3 0.1 copy-done.7
  381.4 2.0 fusion.26
  383.4 0.0 all-gather.13.cloned.1.call-update
  383.4 0.2 all-gather.15.cloned.1.call-start
  383.7 4.4 gather_fusion.8
  388.1 3.7 convolution_bitcast_fusion.2
  391.8 10.3 %all-gather.13.cloned.1.call-done = bf16[32,128,128]{2,1,0:T(8,128)(2,1)} async-done(((bf16[8,128,128]{2,1,0:T(8,128)(2,1)}), bf16[32,128,128]{2,1,0:T(8,128)(2,1)}) %all-gather.13.cloned.1.call-update) | async-done | bytes 1048592 | tf_op jit(solution)/shard_map/all_gather | solution.py:61
  402.1 4.0 gather_fusion.6
  406.1 4.2 fusion.27
  410.3 0.0 all-gather.15.cloned.1.call-update
  410.3 52.1 %all-to-all-done.3 = bf16[1,128,128,128]{3,2,0,1:T(8,128)(2,1)} async-done(((bf16[1,128,128,128]{3,2,0,1:T(8,128)(2,1)}), bf16[1,128,128,128]{3,2,0,1:T(8,128)(2,1)}, u32[]{:S(2)}, u32[]{:S(2)}) %all-to-all-start.3) | async-done | bytes 4194336 | tf_op jit(solution)/shard_map/all_to_all | solution.py:69
  462.4 4.4 gather_fusion.11
  466.7 3.7 convolution_bitcast_fusion
  470.5 3.9 gather_fusion.9
  474.4 4.0 fusion.23
  (24 shorter events, 0.1 us)
Async XLA Ops:
  6.5 134.9 %copy-start = (bf16[8,12,128,128]{3,2,1,0:T(8,128)(2,1)S(1)}, bf16[8,12,128,128]{3,2,1,0:T(8,128)(2,1)}, u32[]{:S(2)}) copy-start(bf16[8,12,128,128]{3,2,1,0:T(8,128)(2,1)} %param.14) | copy-start | bytes 9437188
  6.5 20.5 %all-gather.17.cloned.1.call-start = ((), (), s32[]{:S(2)}) async-start(), calls=%async_computation.8 | async-start | bytes 1310720 | tf_op jit(solution)/shard_map/all_gather | solution.py:64
  35.9 8.4 %copy-start.6 = (s32[8,12]{1,0:T(8,128)S(1)}, s32[8,12]{1,0:T(8,128)}, u32[]{:S(2)}) copy-start(s32[8,12]{1,0:T(8,128)} %param.16) | copy-start | bytes 1156
  35.9 98.1 %all-to-all-start = ((bf16[1,128,128,128]{3,2,0,1:T(8,128)(2,1)}), bf16[1,128,128,128]{3,2,0,1:T(8,128)(2,1)}, u32[]{:S(2)}, u32[]{:S(2)}) async-start(bf16[1,128,128,128]{3,2,0,1:T(8,128)(2,1)} %fusion.3), calls=%async_computation | async-start | bytes 8388608 | tf_op jit(solution)/shard_map/all_to_all | solution.py:69
  41.5 19.7 %all-gather.9.cloned.1.call-start = ((), (), s32[]{:S(2)}) async-start(), calls=%async_computation.4 | async-start | bytes 1310720 | tf_op jit(solution)/shard_map/all_gather | solution.py:61
  43.5 100.1 %all-gather.19.cloned.1.call-start = ((), (), s32[]{:S(2)}) async-start(), calls=%async_computation.9 | async-start | bytes 1310720 | tf_op jit(solution)/shard_map/all_gather | solution.py:64
  44.3 115.7 %all-gather.11.cloned.1.call-start = ((), (), s32[]{:S(2)}) async-start(), calls=%async_computation.5 | async-start | bytes 1310720 | tf_op jit(solution)/shard_map/all_gather | solution.py:61
  138.3 3.2 copy-start.1
  138.3 3.2 copy-start.3
  138.3 3.3 copy-start.4
  138.3 3.3 copy-start.5
  363.7 98.7 %all-to-all-start.3 = ((bf16[1,128,128,128]{3,2,0,1:T(8,128)(2,1)}), bf16[1,128,128,128]{3,2,0,1:T(8,128)(2,1)}, u32[]{:S(2)}, u32[]{:S(2)}) async-start(bf16[1,128,128,128]{3,2,0,1:T(8,128)(2,1)} %get-tuple-element.13), calls=%async_computation.3 | async-start | bytes 8388608 | tf_op jit(solution)/shard_map/all_to_all | solution.py:69
  369.9 32.2 %all-gather.13.cloned.1.call-start = ((), (), s32[]{:S(2)}) async-start(), calls=%async_computation.6 | async-start | bytes 1310720 | tf_op jit(solution)/shard_map/all_gather | solution.py:61
  378.2 3.2 copy-start.2
  378.2 3.2 copy-start.7
  383.4 87.0 %all-gather.15.cloned.1.call-start = ((), (), s32[]{:S(2)}) async-start(), calls=%async_computation.7 | async-start | bytes 1310720 | tf_op jit(solution)/shard_map/all_gather | solution.py:61
Sparse Core Ops, SparseCore 0:
  8.9 18.0 all-gather.16
  43.8 17.2 all-gather.8
  62.7 16.7 all-gather.18
  143.7 16.1 all-gather.10
  383.6 18.5 all-gather.12
  410.4 16.7 all-gather.14
where the time goes:
time: 489 us; the launch traced here: 485 us
  blocking collectives  193 us (39%)
  waiting for transfers between devices  170 us (35%)
  local copies, waits for them, and re-layouts  53.2 us (11%)
  matrix products  25.7 us (5%)
  other arithmetic  17.6 us (4%)
  between operations  13.6 us (3%)
  starting transfers between devices  12.1 us (2%)
    all_to_all x2, blocking collectives, shards(): lax.all_to_all(jnp.where(slot_used[None, :, None, None], picked, jnp.zero...  193 us
    all_to_all x2, waiting for transfers between devices, shards(): lax.all_to_all(jnp.where(slot_used[None, :, None, None], picked, jnp.zero...  121 us
    all_gather x4, waiting for transfers between devices, shards(): section = lax.all_gather(rate_now, 'col', axis=0, tiled=True)  34.8 us
    gather x4, local copies, waits for them, and re-layouts, shards(): arrived[arrival].reshape(row_count, -1, trial_count, block_len)  17.5 us
    gather x4, local copies, waits for them, and re-layouts, shards(): picked = frames[:, slot_place]  17.1 us
    gather x4, local copies, waits for them, and re-layouts, shards(): section[local_index]  15.8 us
    all_gather x2, waiting for transfers between devices, shards(): source = lax.all_gather(past_rates[step_idx], 'col', axis=0, tiled=True)  14 us
    dot_general x4, matrix products, shards(): jnp.einsum('rktb,rkob->rto', arrived[arrival].reshape(row_count, -1, tria...  13.6 us
  transfers between devices with their start and end apart: 8, of which 6 were waited for; matrix products, arithmetic and copies ran while one was open for 14% of the time, Pallas kernels for 0%

commit v1 on v0

--- a/solution.py
+++ b/solution.py
@@ -1,12 +1,20 @@
+import functools
+
 import jax
 import jax.numpy as jnp
 from jax import lax
 from jax.sharding import PartitionSpec as P
 
+from jax.experimental import pallas as pl
+from jax.experimental.pallas import tpu as pltpu
+
 STEPS = 4
-
-
-def shards(
+CORES = 2
+PLANE = 2
+VMEM_GRANT = 60 * 1024 * 1024
+
+
+def shards_exchange(
     initial_state,
     past_rates,
     stimulus,
@@ -88,6 +96,324 @@
     return membrane
 
 
+def softplus(values):
+    return jnp.maximum(values, 0.0) + jnp.log1p(jnp.exp(-jnp.abs(values)))
+
+
+def kernel(
+    dims,
+    far_idx,
+    local_idx,
+    initial,
+    stimulus,
+    leak,
+    past,
+    local_weight,
+    far_weight,
+    out,
+    *scratch,
+):
+    depth_len, rows = dims
+    delay_len = past.shape[0]
+    frame_count = STEPS
+    far_frames = scratch[:frame_count]
+    near_frames = scratch[frame_count : 2 * frame_count + delay_len]
+    near_weight, distant_weight, load_sem, send_sem, recv_sem = scratch[2 * frame_count + delay_len :]
+    my_area = lax.axis_index("area")
+    my_col = lax.axis_index("col")
+    my_depth, my_x = my_area // PLANE, my_area % PLANE
+    my_y, my_core = my_col // CORES, my_col % CORES
+    other_x, other_y, other_core = 1 - my_x, 1 - my_y, 1 - my_core
+    col_count = lax.axis_size("col")
+    half = rows // 2
+
+    def area_at(depth_back, x_pos):
+        return lax.rem(my_depth - depth_back + depth_len, depth_len) * PLANE + x_pos
+
+    to_x = {"area": my_depth * PLANE + other_x, "col": my_col}
+    to_y = {"area": my_area, "col": other_y * CORES + my_core}
+    to_core = {"area": my_area, "col": my_y * CORES + other_core}
+
+    def to_depth(step):
+        return {"area": lax.rem(my_depth + step, depth_len) * PLANE + my_x, "col": my_col}
+
+    partners = [to_depth(step) for step in range(1, depth_len)] + [to_x, to_y, to_core]
+
+    loads = [
+        pltpu.make_async_copy(
+            past.at[index], near_frames[index].at[pl.ds(my_col * rows, rows)], load_sem.at[index]
+        )
+        for index in range(delay_len)
+    ]
+    loads.append(pltpu.make_async_copy(local_weight, near_weight, load_sem.at[delay_len]))
+    loads.append(pltpu.make_async_copy(far_weight, distant_weight, load_sem.at[delay_len + 1]))
+    for load in loads:
+        load.start()
+
+    barrier = pltpu.get_barrier_semaphore()
+    for partner in partners:
+        pl.semaphore_signal(barrier, inc=1, device_id=partner, device_id_type=pl.DeviceIdType.MESH)
+
+    def prepare(row, carry):
+        state = initial[row]
+        out[row] = state
+        near_frames[delay_len][my_col * rows + row] = softplus(state).astype(jnp.bfloat16)
+        return carry
+
+    lax.fori_loop(0, rows, prepare, 0)
+    pl.semaphore_wait(barrier, len(partners))
+    for load in loads[:delay_len]:
+        load.wait()
+
+    started = {}
+    numbers = {}
+
+    def near_view(frame, y_pos, core, first=0, count=None):
+        start = (y_pos * CORES + core) * rows + first
+        return near_frames[frame].at[pl.ds(start, rows if count is None else count)]
+
+    def far_view(frame, area, y_pos, core, first=0, count=None):
+        start = (area * col_count + y_pos * CORES + core) * rows + first
+        return far_frames[frame].at[pl.ds(start, rows if count is None else count)]
+
+    def send(key, source, target, device):
+        number = numbers.setdefault(key, len(numbers))
+        copy = pltpu.make_async_remote_copy(
+            src_ref=source,
+            dst_ref=target,
+            send_sem=send_sem.at[number],
+            recv_sem=recv_sem.at[number],
+            device_id=device,
+            device_id_type=pl.DeviceIdType.MESH,
+        )
+        copy.start()
+        started[key] = copy
+
+    def arrived(key):
+        started[key].wait_recv()
+
+    def own_depth(frame):
+        mine = near_view(frame, my_y, my_core)
+        for step in range(1, depth_len):
+            send(("z", frame, step), mine, far_view(frame, my_area, my_y, my_core), to_depth(step))
+
+    def own_x(frame):
+        mine = near_view(frame, my_y, my_core)
+        send(("x", frame, 0), mine, far_view(frame, my_area, my_y, my_core), to_x)
+
+    def own_section(frame):
+        if frame < delay_len:
+            part = near_view(frame, my_y, my_core, half, rows - half)
+            send(("y", frame, 0), part, part, to_y)
+        else:
+            mine = near_view(frame, my_y, my_core)
+            send(("y", frame, 0), mine, mine, to_y)
+            send(("c", frame), mine, mine, to_core)
+
+    def column(frame):
+        for step in range(1, depth_len):
+            arrived(("z", frame, step))
+            view = far_view(frame, area_at(step, my_x), my_y, my_core)
+            send(("x", frame, step), view, view, to_x)
+            send(("y", frame, step), view, view, to_y)
+            send(("cz", frame, step), view, view, to_core)
+
+    def section_arrival(frame):
+        arrived(("y", frame, 0))
+        view = near_view(frame, other_y, my_core)
+        send(("cy", frame, 0), view, view, to_core)
+
+    def section_ready(frame):
+        arrived(("c", frame))
+        arrived(("cy", frame, 0))
+
+    def relay(frame):
+        for step in range(depth_len):
+            arrived(("x", frame, step))
+            area = area_at(step, other_x)
+            part = far_view(frame, area, my_y, my_core, 0, half)
+            send(("dy", frame, step), part, part, to_y)
+            view = far_view(frame, area, my_y, my_core)
+            send(("cx", frame, step), view, view, to_core)
+            area = area_at(step, my_x)
+            if step == 0:
+                if frame < delay_len:
+                    arrived(("y", frame, 0))
+                part = near_view(frame, other_y, my_core, half, rows - half)
+                send(
+                    ("dx", frame, step),
+                    part,
+                    far_view(frame, area, other_y, my_core, half, rows - half),
+                    to_x,
+                )
+            else:
+                arrived(("y", frame, step))
+                part = far_view(frame, area, other_y, my_core, half, rows - half)
+                send(("dx", frame, step), part, part, to_x)
+                view = far_view(frame, area, other_y, my_core)
+                send(("cy", frame, step), view, view, to_core)
+
+    def diagonal(frame):
+        for step in range(depth_len):
+            arrived(("dy", frame, step))
+            arrived(("dx", frame, step))
+            view = far_view(frame, area_at(step, other_x), other_y, my_core)
+            send(("cd", frame, step), view, view, to_core)
+
+    def frame_ready(frame):
+        for step in range(depth_len):
+            if step > 0:
+                arrived(("cz", frame, step))
+                arrived(("cy", frame, step))
+            arrived(("cx", frame, step))
+            arrived(("cd", frame, step))
+
+    def products(blocks, index, weights, row):
+        listed = jnp.concatenate(
+            [blocks[index[row, link]] for link in range(index.shape[1])], axis=1
+        )
+        kernel_row = jnp.concatenate(
+            [weights[row, link] for link in range(index.shape[1])], axis=1
+        )
+        return lax.dot_general(
+            listed, kernel_row, (((1,), (1,)), ((), ())), preferred_element_type=jnp.float32
+        )
+
+    def euler(step):
+        def one_row(row, carry):
+            lateral = products(near_frames[step + delay_len], local_idx, near_weight, row)
+            distant = products(far_frames[step], far_idx, distant_weight, row)
+            state = out[row]
+            drive = stimulus[row].astype(jnp.float32)
+            state = state + leak[pl.ds(row, 1), :] * (-state + lateral + distant + drive)
+            out[row] = state
+            if step + 1 < STEPS:
+                near_frames[step + delay_len + 1][my_col * rows + row] = softplus(state).astype(
+                    jnp.bfloat16
+                )
+            return carry
+
+        lax.fori_loop(0, rows, one_row, 0)
+
+    own_section(delay_len)
+    own_depth(0)
+    own_x(0)
+    own_section(0)
+    column(0)
+    for frame in range(1, delay_len):
+        own_depth(frame)
+        own_x(frame)
+        own_section(frame)
+    section_arrival(delay_len)
+    own_depth(delay_len)
+    own_x(delay_len)
+    for frame in range(1, delay_len):
+        column(frame)
+    relay(0)
+    diagonal(0)
+    for load in loads[delay_len:]:
+        load.wait()
+    for step in range(STEPS):
+        if step > 0:
+            relay(step)
+            diagonal(step)
+        frame = step + delay_len
+        if step > 0:
+            section_arrival(frame)
+        section_ready(frame)
+        frame_ready(step)
+        euler(step)
+        following = frame + 1
+        if step + 1 < STEPS:
+            own_section(following)
+            if following < frame_count:
+                own_depth(following)
+                own_x(following)
+        if frame < frame_count:
+            column(frame)
+    for copy in started.values():
+        copy.wait_send()
+
+
+def shards_gather(
+    initial_state,
+    past_rates,
+    stimulus,
+    leak_rate,
+    local_weight,
+    far_weight,
+    local_index,
+    area_sizes,
+    far_area,
+    far_offset,
+):
+    area_count = lax.axis_size("area")
+    col_count = lax.axis_size("col")
+    rows, trials, block_len = initial_state.shape
+    first_row = (lax.axis_index("area") * col_count + lax.axis_index("col")) * rows
+    delay_len = past_rates.shape[0]
+    section_len = rows * col_count
+    block_count = section_len * area_count
+    my_areas = lax.dynamic_slice_in_dim(far_area, first_row, rows)
+    my_offsets = lax.dynamic_slice_in_dim(far_offset, first_row, rows)
+    area_len = jnp.zeros_like(my_areas)
+    area_first = jnp.zeros_like(my_areas)
+    for area in range(area_sizes.shape[0]):
+        area_len = area_len + jnp.where(my_areas == area, area_sizes[area], 0)
+        area_first = area_first + jnp.where(my_areas > area, area_sizes[area], 0)
+    far_block = area_first * section_len + my_offsets % (area_len * section_len)
+    depth_len = area_count // PLANE
+    copies = copy_count(depth_len, STEPS, delay_len)
+    block = (trials, block_len)
+    vmem = pl.BlockSpec(memory_space=pltpu.VMEM)
+    smem = pl.BlockSpec(memory_space=pltpu.SMEM)
+    hbm = pl.BlockSpec(memory_space=pl.ANY)
+    links = local_weight.shape[1] + far_weight.shape[1]
+    return pl.pallas_call(
+        functools.partial(kernel, (depth_len, rows)),
+        out_shape=jax.ShapeDtypeStruct(initial_state.shape, jnp.float32),
+        in_specs=[smem, smem, vmem, vmem, vmem, hbm, hbm, hbm],
+        out_specs=vmem,
+        scratch_shapes=[pltpu.VMEM((block_count,) + block, jnp.bfloat16) for _ in range(STEPS)]
+        + [pltpu.VMEM((section_len,) + block, jnp.bfloat16) for _ in range(STEPS + delay_len)]
+        + [
+            pltpu.VMEM(local_weight.shape, jnp.bfloat16),
+            pltpu.VMEM(far_weight.shape, jnp.bfloat16),
+            pltpu.SemaphoreType.DMA((delay_len + 2,)),
+            pltpu.SemaphoreType.DMA((copies,)),
+            pltpu.SemaphoreType.DMA((copies,)),
+        ],
+        compiler_params=pltpu.CompilerParams(
+            collective_id=0, has_side_effects=True, vmem_limit_bytes=VMEM_GRANT
+        ),
+        cost_estimate=pl.CostEstimate(
+            flops=2 * STEPS * rows * links * trials * block_len * block_len,
+            bytes_accessed=2 * rows * (links + 8) * trials * block_len,
+            transcendentals=2 * STEPS * rows * trials * block_len,
+        ),
+    )(far_block, local_index, initial_state, stimulus, leak_rate, past_rates, local_weight, far_weight)
+
+
+def copy_count(depth_len, steps, delay_len):
+    per_frame = 3 * (depth_len - 1) + 6 * depth_len
+    return steps * per_frame + 3 * steps
+
+
+def shards(*arrays):
+    initial_state, past_rates = arrays[0], arrays[1]
+    area_count = lax.axis_size("area")
+    col_count = lax.axis_size("col")
+    shard_bytes = past_rates[0].size * past_rates.dtype.itemsize
+    held = STEPS * shard_bytes * area_count * col_count
+    held += (STEPS + past_rates.shape[0]) * shard_bytes * col_count
+    held += sum(array.size * array.dtype.itemsize for array in arrays[4:6])
+    held += 3 * initial_state.size * initial_state.dtype.itemsize
+    planar = col_count == CORES * 2 and area_count % PLANE == 0 and initial_state.shape[0] % 2 == 0
+    if planar and held < VMEM_GRANT:
+        return shards_gather(*arrays)
+    return shards_exchange(*arrays)
+
+
 def solution(mesh):
     return jax.shard_map(
         shards,

time: 489 us -> 203 us (0.42)
  Pallas kernels: 0 us -> 195 us
  blocking collectives: 193 us -> 0 us
  waiting for transfers between devices: 170 us -> 0 us
  local copies, waits for them, and re-layouts: 53.2 us -> 4.24 us
  matrix products: 25.7 us -> 0 us
  other arithmetic: 17.6 us -> 3.21 us
  between operations: 13.6 us -> 0.01 us
  starting transfers between devices: 12.1 us -> 0 us
    pallas_call x0 -> x1, Pallas kernels: none -> 195 us  [shards_gather(): pl.pallas_call(functools.partial(kernel, (depth_len, rows)), out_shape=ja...]
    all_to_all x2 -> x0, blocking collectives: 193 us -> none  [shards(): lax.all_to_all(jnp.where(slot_used[None, :, None, None], picked, jnp.zero...]
    all_to_all x2 -> x0, waiting for transfers between devices: 121 us -> none  [shards(): lax.all_to_all(jnp.where(slot_used[None, :, None, None], picked, jnp.zero...]
    gather x12 -> x0, local copies, waits for them, and re-layouts: 50.3 us -> none  [the longest x4 17.5 us: shards(): arrived[arrival].reshape(row_count, -1, trial_count, block_len)]
    all_gather x6 -> x0, waiting for transfers between devices: 48.8 us -> none  [the longest x4 34.8 us: shards(): section = lax.all_gather(rate_now, 'col', axis=0, tiled=True)]
    dot_general x8 -> x0, matrix products: 25.7 us -> none  [the longest x4 13.6 us: shards(): jnp.einsum('rktb,rkob->rto', arrived[arrival].reshape(row_count, -1, tria...]
    all_to_all x2 -> x0, starting transfers between devices: 11.8 us -> none  [shards(): lax.all_to_all(jnp.where(slot_used[None, :, None, None], picked, jnp.zero...]
    select_n x7 -> x0, other arithmetic: 11.6 us -> none  [the longest x2 11.5 us: shards(): jnp.where(slot_used[None, :, None, None], picked, jnp.zeros((), frames.dt...]
  transfers between devices with their start and end apart: 8 -> 0, of which waited for: 6 -> 0; matrix products, arithmetic and copies ran while one was open for 14% -> 0% of each run, Pallas kernels for 0% -> 0%
where the time goes in v1:
time: 203 us
  Pallas kernels  195 us (96%)
  local copies, waits for them, and re-layouts  4.24 us (2%)
  other arithmetic  3.21 us (2%)
    pallas_call x1, Pallas kernels, shards_gather(): pl.pallas_call(functools.partial(kernel, (depth_len, rows)), out_shape=ja...  195 us

profile of v1, /device:TPU:25, one launch (start us, length us, event | category | flops | bytes accessed | tf_op | source)
XLA Modules:
  0.0 202.5 jit_solution(9140579458407544656)
XLA Ops:
  0.0 1.4 fusion.1
  1.5 0.8 constant_dynamic-slice_fusion
  2.2 0.1 copy.14
  2.3 0.1 copy.13
  2.4 3.2 %fusion.far_idx = s32[8,8]{1,0:T(8,128)} fusion(s32[8,8]{1,0:T(8,128)S(1)} %copy.14, s32[8,8]{1,0:T(8,128)S(1)} %copy.13, s32[]{:T(128)} %bitcast.3, s32[]{:T(128)} %bitcast.2, s32[]{:T(128)} %bitcast.1, s32[]{:T(128)} %bitcast), kind=kLoop, calls=%fused_computation.2 | loop fusion | flops 2240 | bytes 784 | tf_op jit(solution)/shard_map/add | solution.py:364
  5.6 195.1 %shard_map.100 = f32[8,128,128]{2,1,0:T(8,128)} custom-call(s32[8,8]{1,0:T(8,128)} %fusion.far_idx, s32[8,12]{1,0:T(8,128)} %local_idx.1, f32[8,128,128]{2,1,0:T(8,128)} %initial.1, bf16[8,128,128]{2,1,0:T(8,128)(2,1)} %stimulus.1, f32[8,128]{1,0:T(8,128)} %leak.1, bf16[2,8,128,128]{3,2,1,0:T(8,128)(2,1)} %past.1, bf16[8,12,128,128]{3,2,1,0:T(8,128)(2,1)} %local_weight.1, ...), custom_call_target="tpu_custom_call" | custom-call | flops 2684354560 | bytes 7340032 | tf_op jit(solution)/shard_map/pallas_call | solution.py:372
  200.7 1.9 copy.16

commit v2 on v1

--- a/solution.py
+++ b/solution.py
@@ -118,7 +118,9 @@
     frame_count = STEPS
     far_frames = scratch[:frame_count]
     near_frames = scratch[frame_count : 2 * frame_count + delay_len]
-    near_weight, distant_weight, load_sem, send_sem, recv_sem = scratch[2 * frame_count + delay_len :]
+    near_weight, distant_weight, lateral_sum, load_sem, send_sem, recv_sem = scratch[
+        2 * frame_count + delay_len :
+    ]
     my_area = lax.axis_index("area")
     my_col = lax.axis_index("col")
     my_depth, my_x = my_area // PLANE, my_area % PLANE
@@ -126,16 +128,26 @@
     other_x, other_y, other_core = 1 - my_x, 1 - my_y, 1 - my_core
     col_count = lax.axis_size("col")
     half = rows // 2
-
-    def area_at(depth_back, x_pos):
-        return lax.rem(my_depth - depth_back + depth_len, depth_len) * PLANE + x_pos
+    carried = max(1, rows // 8)
+    direct = rows - carried
+
+    def paired(step):
+        depth, bit = my_depth, 1
+        while bit <= step:
+            if step // bit % 2:
+                depth = depth + bit - 2 * bit * ((depth // bit) % 2)
+            bit *= 2
+        return depth
+
+    def area_at(step, x_pos):
+        return paired(step) * PLANE + x_pos
 
     to_x = {"area": my_depth * PLANE + other_x, "col": my_col}
     to_y = {"area": my_area, "col": other_y * CORES + my_core}
     to_core = {"area": my_area, "col": my_y * CORES + other_core}
 
     def to_depth(step):
-        return {"area": lax.rem(my_depth + step, depth_len) * PLANE + my_x, "col": my_col}
+        return {"area": area_at(step, my_x), "col": my_col}
 
     partners = [to_depth(step) for step in range(1, depth_len)] + [to_x, to_y, to_core]
 
@@ -154,16 +166,15 @@
     for partner in partners:
         pl.semaphore_signal(barrier, inc=1, device_id=partner, device_id_type=pl.DeviceIdType.MESH)
 
+    pl.semaphore_wait(barrier, len(partners))
+    for load in loads[:delay_len]:
+        load.wait()
+
     def prepare(row, carry):
         state = initial[row]
         out[row] = state
         near_frames[delay_len][my_col * rows + row] = softplus(state).astype(jnp.bfloat16)
         return carry
-
-    lax.fori_loop(0, rows, prepare, 0)
-    pl.semaphore_wait(barrier, len(partners))
-    for load in loads[:delay_len]:
-        load.wait()
 
     started = {}
     numbers = {}
@@ -210,13 +221,13 @@
             send(("y", frame, 0), mine, mine, to_y)
             send(("c", frame), mine, mine, to_core)
 
-    def column(frame):
-        for step in range(1, depth_len):
-            arrived(("z", frame, step))
-            view = far_view(frame, area_at(step, my_x), my_y, my_core)
-            send(("x", frame, step), view, view, to_x)
-            send(("y", frame, step), view, view, to_y)
-            send(("cz", frame, step), view, view, to_core)
+    def column(frame, step):
+        arrived(("z", frame, step))
+        view = far_view(frame, area_at(step, my_x), my_y, my_core)
+        part = far_view(frame, area_at(step, my_x), my_y, my_core, 0, direct)
+        send(("x", frame, step), part, part, to_x)
+        send(("y", frame, step), part, part, to_y)
+        send(("cz", frame, step), view, view, to_core)
 
     def section_arrival(frame):
         arrived(("y", frame, 0))
@@ -227,38 +238,45 @@
         arrived(("c", frame))
         arrived(("cy", frame, 0))
 
-    def relay(frame):
-        for step in range(depth_len):
-            arrived(("x", frame, step))
-            area = area_at(step, other_x)
-            part = far_view(frame, area, my_y, my_core, 0, half)
-            send(("dy", frame, step), part, part, to_y)
-            view = far_view(frame, area, my_y, my_core)
-            send(("cx", frame, step), view, view, to_core)
-            area = area_at(step, my_x)
-            if step == 0:
-                if frame < delay_len:
-                    arrived(("y", frame, 0))
-                part = near_view(frame, other_y, my_core, half, rows - half)
-                send(
-                    ("dx", frame, step),
-                    part,
-                    far_view(frame, area, other_y, my_core, half, rows - half),
-                    to_x,
-                )
-            else:
-                arrived(("y", frame, step))
-                part = far_view(frame, area, other_y, my_core, half, rows - half)
-                send(("dx", frame, step), part, part, to_x)
-                view = far_view(frame, area, other_y, my_core)
-                send(("cy", frame, step), view, view, to_core)
-
-    def diagonal(frame):
-        for step in range(depth_len):
-            arrived(("dy", frame, step))
-            arrived(("dx", frame, step))
-            view = far_view(frame, area_at(step, other_x), other_y, my_core)
-            send(("cd", frame, step), view, view, to_core)
+    def relay(frame, step):
+        arrived(("x", frame, step))
+        area = area_at(step, other_x)
+        part = far_view(frame, area, my_y, my_core, 0, half)
+        send(("dy", frame, step), part, part, to_y)
+        if step > 0:
+            arrived(("zx", frame, step))
+        view = far_view(frame, area, my_y, my_core)
+        send(("cx", frame, step), view, view, to_core)
+        area = area_at(step, my_x)
+        if step == 0:
+            if frame < delay_len:
+                arrived(("y", frame, 0))
+            part = near_view(frame, other_y, my_core, half, rows - half)
+            send(
+                ("dx", frame, step),
+                part,
+                far_view(frame, area, other_y, my_core, half, rows - half),
+                to_x,
+            )
+            for other in range(1, depth_len):
+                part = far_view(frame, my_depth * PLANE + other_x, my_y, my_core, direct, carried)
+                send(("zx", frame, other), part, part, to_depth(other))
+                part = near_view(frame, other_y, my_core, direct, carried)
+                target = far_view(frame, my_area, other_y, my_core, direct, carried)
+                send(("zy", frame, other), part, target, to_depth(other))
+        else:
+            arrived(("y", frame, step))
+            arrived(("zy", frame, step))
+            part = far_view(frame, area, other_y, my_core, half, rows - half)
+            send(("dx", frame, step), part, part, to_x)
+            view = far_view(frame, area, other_y, my_core)
+            send(("cy", frame, step), view, view, to_core)
+
+    def diagonal(frame, step):
+        arrived(("dy", frame, step))
+        arrived(("dx", frame, step))
+        view = far_view(frame, area_at(step, other_x), other_y, my_core)
+        send(("cd", frame, step), view, view, to_core)
 
     def frame_ready(frame):
         for step in range(depth_len):
@@ -279,13 +297,20 @@
             listed, kernel_row, (((1,), (1,)), ((), ())), preferred_element_type=jnp.float32
         )
 
+    def add_lateral(step):
+        def one_row(row, carry):
+            lateral_sum[row] = products(near_frames[step + delay_len], local_idx, near_weight, row)
+            return carry
+
+        lax.fori_loop(0, rows, one_row, 0)
+
     def euler(step):
         def one_row(row, carry):
-            lateral = products(near_frames[step + delay_len], local_idx, near_weight, row)
             distant = products(far_frames[step], far_idx, distant_weight, row)
             state = out[row]
             drive = stimulus[row].astype(jnp.float32)
-            state = state + leak[pl.ds(row, 1), :] * (-state + lateral + distant + drive)
+            change = -state + lateral_sum[row] + distant + drive
+            state = state + leak[pl.ds(row, 1), :] * change
             out[row] = state
             if step + 1 < STEPS:
                 near_frames[step + delay_len + 1][my_col * rows + row] = softplus(state).astype(
@@ -295,42 +320,48 @@
 
         lax.fori_loop(0, rows, one_row, 0)
 
-    own_section(delay_len)
+    steps = range(1, depth_len)
     own_depth(0)
-    own_x(0)
-    own_section(0)
-    column(0)
-    for frame in range(1, delay_len):
-        own_depth(frame)
+    for frame in range(delay_len):
         own_x(frame)
         own_section(frame)
+    lax.fori_loop(0, rows, prepare, 0)
+    own_section(delay_len)
+    own_x(delay_len)
+    column(0, 1)
+    relay(0, 0)
+    for step in range(2, depth_len):
+        column(0, step)
+    own_depth(1)
     section_arrival(delay_len)
-    own_depth(delay_len)
-    own_x(delay_len)
-    for frame in range(1, delay_len):
-        column(frame)
-    relay(0)
-    diagonal(0)
-    for load in loads[delay_len:]:
-        load.wait()
+    for frame in (*range(1, delay_len), delay_len):
+        relay(frame, 0)
     for step in range(STEPS):
-        if step > 0:
-            relay(step)
-            diagonal(step)
         frame = step + delay_len
+        if step == 0:
+            for load in loads[delay_len:]:
+                load.wait()
+        for part in steps:
+            if step + 1 < frame_count:
+                column(step + 1, part)
+            if step == 0 and part + 1 == depth_len:
+                own_depth(delay_len)
+            relay(step, part)
         if step > 0:
             section_arrival(frame)
+            if delay_len < frame < frame_count:
+                relay(frame, 0)
         section_ready(frame)
+        add_lateral(step)
+        for part in range(depth_len):
+            diagonal(step, part)
         frame_ready(step)
         euler(step)
-        following = frame + 1
         if step + 1 < STEPS:
-            own_section(following)
-            if following < frame_count:
-                own_depth(following)
-                own_x(following)
-        if frame < frame_count:
-            column(frame)
+            own_section(frame + 1)
+            if frame + 1 < frame_count:
+                own_depth(frame + 1)
+                own_x(frame + 1)
     for copy in started.values():
         copy.wait_send()
 
@@ -361,7 +392,11 @@
     for area in range(area_sizes.shape[0]):
         area_len = area_len + jnp.where(my_areas == area, area_sizes[area], 0)
         area_first = area_first + jnp.where(my_areas > area, area_sizes[area], 0)
-    far_block = area_first * section_len + my_offsets % (area_len * section_len)
+    span = area_len * section_len
+    turns = (my_offsets.astype(jnp.float32) / span.astype(jnp.float32)).astype(jnp.int32)
+    place = my_offsets - turns * span
+    place = jnp.where(place < 0, place + span, jnp.where(place >= span, place - span, place))
+    far_block = area_first * section_len + place
     depth_len = area_count // PLANE
     copies = copy_count(depth_len, STEPS, delay_len)
     block = (trials, block_len)
@@ -379,6 +414,7 @@
         + [
             pltpu.VMEM(local_weight.shape, jnp.bfloat16),
             pltpu.VMEM(far_weight.shape, jnp.bfloat16),
+            pltpu.VMEM(initial_state.shape, jnp.float32),
             pltpu.SemaphoreType.DMA((delay_len + 2,)),
             pltpu.SemaphoreType.DMA((copies,)),
             pltpu.SemaphoreType.DMA((copies,)),
@@ -391,11 +427,20 @@
             bytes_accessed=2 * rows * (links + 8) * trials * block_len,
             transcendentals=2 * STEPS * rows * trials * block_len,
         ),
-    )(far_block, local_index, initial_state, stimulus, leak_rate, past_rates, local_weight, far_weight)
+    )(
+        far_block,
+        local_index,
+        initial_state,
+        stimulus,
+        leak_rate,
+        past_rates,
+        local_weight,
+        far_weight,
+    )
 
 
 def copy_count(depth_len, steps, delay_len):
-    per_frame = 3 * (depth_len - 1) + 6 * depth_len
+    per_frame = 5 * (depth_len - 1) + 6 * depth_len
     return steps * per_frame + 3 * steps
 
 
@@ -409,6 +454,8 @@
     held += sum(array.size * array.dtype.itemsize for array in arrays[4:6])
     held += 3 * initial_state.size * initial_state.dtype.itemsize
     planar = col_count == CORES * 2 and area_count % PLANE == 0 and initial_state.shape[0] % 2 == 0
+    depth_len = area_count // PLANE
+    planar = planar and depth_len & (depth_len - 1) == 0
     if planar and held < VMEM_GRANT:
         return shards_gather(*arrays)
     return shards_exchange(*arrays)

time: 203 us -> 181 us (0.89)
  the two profiles are of different devices: /device:TPU:25 before, /device:TPU:17 now
where the time goes in v2:
time: 181 us
  Pallas kernels  173 us (96%)
  local copies, waits for them, and re-layouts  4.24 us (2%)
  other arithmetic  3.1 us (2%)
    pallas_call x1, Pallas kernels, shards_gather(): pl.pallas_call(functools.partial(kernel, (depth_len, rows)), out_shape=ja...  173 us

profile of v2, /device:TPU:17, one launch (start us, length us, event | category | flops | bytes accessed | tf_op | source)
XLA Modules:
  0.0 180.7 jit_solution(8468278078929795334)
XLA Ops:
  0.0 1.4 fusion.2
  1.5 0.8 constant_dynamic-slice_fusion
  2.2 0.1 copy.14
  2.3 0.1 copy.13
  2.4 3.1 %fusion.1.far_idx = s32[8,8]{1,0:T(8,128)} fusion(s32[8,8]{1,0:T(8,128)S(1)} %copy.14, s32[8,8]{1,0:T(8,128)S(1)} %copy.13, s32[]{:T(128)} %bitcast.3, s32[]{:T(128)} %bitcast.2, s32[]{:T(128)} %bitcast.1, s32[]{:T(128)} %bitcast), kind=kLoop, calls=%fused_computation.2 | loop fusion | flops 2368 | bytes 784 | tf_op jit(solution)/shard_map/add | solution.py:399
  5.5 173.4 %shard_map.100 = f32[8,128,128]{2,1,0:T(8,128)} custom-call(s32[8,8]{1,0:T(8,128)} %fusion.1.far_idx, s32[8,12]{1,0:T(8,128)} %local_idx.1, f32[8,128,128]{2,1,0:T(8,128)} %initial.1, bf16[8,128,128]{2,1,0:T(8,128)(2,1)} %stimulus.1, f32[8,128]{1,0:T(8,128)} %leak.1, bf16[2,8,128,128]{3,2,1,0:T(8,128)(2,1)} %past.1, bf16[8,12,128,128]{3,2,1,0:T(8,128)(2,1)} %local_weight.1, ...), custom_call_target="tpu_custom_call" | custom-call | flops 2684354560 | bytes 7340032 | tf_op jit(solution)/shard_map/pallas_call | solution.py:407
  178.9 1.9 %copy.16 = f32[8,128,128]{2,1,0:T(8,128)} copy(f32[8,128,128]{2,1,0:T(8,128)} %shard_map.100) | data formatting | bytes 1048576

commit v3 on v2

--- a/solution.py
+++ b/solution.py
@@ -320,6 +320,13 @@
 
         lax.fori_loop(0, rows, one_row, 0)
 
+    issued = set()
+
+    def once(action, frame, part):
+        if (action, frame, part) not in issued:
+            issued.add((action, frame, part))
+            action(frame, part)
+
     steps = range(1, depth_len)
     own_depth(0)
     for frame in range(delay_len):
@@ -342,16 +349,21 @@
             for load in loads[delay_len:]:
                 load.wait()
         for part in steps:
+            once(relay, step, part)
             if step + 1 < frame_count:
-                column(step + 1, part)
-            if step == 0 and part + 1 == depth_len:
+                once(column, step + 1, part)
+            if step == 0 and part == 1:
                 own_depth(delay_len)
-            relay(step, part)
         if step > 0:
             section_arrival(frame)
             if delay_len < frame < frame_count:
                 relay(frame, 0)
         section_ready(frame)
+        if step + 2 < frame_count:
+            for part in steps[:-1]:
+                once(column, step + 2, part)
+        if step + 1 < frame_count:
+            once(relay, step + 1, 1)
         add_lateral(step)
         for part in range(depth_len):
             diagonal(step, part)

time: 181 us -> 171 us (0.945)
  the two profiles are of different devices: /device:TPU:17 before, /device:TPU:25 now
where the time goes in v3:
time: 171 us; the launch traced here: 169 us
  Pallas kernels  162 us (95%)
  local copies, waits for them, and re-layouts  4.24 us (2%)
  other arithmetic  3.1 us (2%)
    pallas_call x1, Pallas kernels, shards_gather(): pl.pallas_call(functools.partial(kernel, (depth_len, rows)), out_shape=ja...  162 us

profile of v3, /device:TPU:25, one launch (start us, length us, event | category | flops | bytes accessed | tf_op | source)
XLA Modules:
  0.0 169.1 jit_solution(10549941940480189779)
XLA Ops:
  0.0 1.4 fusion.2
  1.5 0.8 constant_dynamic-slice_fusion
  2.2 0.1 copy.14
  2.3 0.1 copy.13
  2.4 3.1 %fusion.1.far_idx = s32[8,8]{1,0:T(8,128)} fusion(s32[8,8]{1,0:T(8,128)S(1)} %copy.14, s32[8,8]{1,0:T(8,128)S(1)} %copy.13, s32[]{:T(128)} %bitcast.3, s32[]{:T(128)} %bitcast.2, s32[]{:T(128)} %bitcast.1, s32[]{:T(128)} %bitcast), kind=kLoop, calls=%fused_computation.2 | loop fusion | flops 2368 | bytes 784 | tf_op jit(solution)/shard_map/add | solution.py:411
  5.5 161.7 %shard_map.100 = f32[8,128,128]{2,1,0:T(8,128)} custom-call(s32[8,8]{1,0:T(8,128)} %fusion.1.far_idx, s32[8,12]{1,0:T(8,128)} %local_idx.1, f32[8,128,128]{2,1,0:T(8,128)} %initial.1, bf16[8,128,128]{2,1,0:T(8,128)(2,1)} %stimulus.1, f32[8,128]{1,0:T(8,128)} %leak.1, bf16[2,8,128,128]{3,2,1,0:T(8,128)(2,1)} %past.1, bf16[8,12,128,128]{3,2,1,0:T(8,128)(2,1)} %local_weight.1, ...), custom_call_target="tpu_custom_call" | custom-call | flops 2684354560 | bytes 7340032 | tf_op jit(solution)/shard_map/pallas_call | solution.py:419
  167.2 1.9 %copy.16 = f32[8,128,128]{2,1,0:T(8,128)} copy(f32[8,128,128]{2,1,0:T(8,128)} %shard_map.100) | data formatting | bytes 1048576
